TPU v7x, 32 devices: a whole 2x2x4 slice. The times are simulated.
32 devices in a mesh: groups: 2 (over y), task: 4 (over x, core), tensor: 4 (over z).
Axes of the slice: x: 2, y: 2, z: 4, core: 2. Of those that a mesh axis runs over, the one named last changes fastest.
Arguments:
- attention: bfloat16 [4096, 8192], P(('groups', 'task'), 'tensor'), parts along dimension 0, may hold values from -6 to 6
- out_weight: bfloat16 [8192, 5120], P('tensor'), may hold values from -0.09375 to 0.09375
- task_tags: int32 [4096], P(('groups', 'task')), parts along dimension 0, may hold values from 0 to 63, as said below
- delta_values: bfloat16 [64, 8, 128, 128], P('task', 'tensor'), may hold values from -0.5 to 0.5
- block_rows: int32 [64, 8], P('task', 'tensor'), may hold values from 0 to 15
- block_columns: int32 [64, 8], P('task', 'tensor'), may hold values from 0 to 39
- block_live: int32 [64, 8], P('task', 'tensor'), may hold values 0 or 1
Outputs:
- projected: bfloat16 [4096, 5120], P(('groups', 'task'), 'tensor'), parts along dimension 0
There are 2 independent parts, one for each index of `groups`. A program takes and returns all parts, laid end to end along the dimension named above; an argument that names none is the same for every part. Nothing has to cross between parts.
Inputs may be any that keep to these rules, and one draw needn't show every extreme that they name: `task_tags`: the tasks form owner groups of 64 / (size of axis task) consecutive tasks. Each device's 512 rows name tasks of any one owner group at most 192 times, and one owner group, the same for every device's rows, exactly 192 times.
All inputs are finite; a program needn't handle non-finite values. No bound on the sum of `block_live` on one device may be relied on, other than what follows from the above.
Results may differ from a plain program's by a relative error of at most 0.001.
Values may be sent and summed in bfloat16 or wider, within the bound.
A program may use at most 128 MiB of HBM per device.

v0:
```python
import jax
import jax.numpy as jnp
from jax import lax
from jax.sharding import PartitionSpec as P


def pick(lookup, onehot):
    return jnp.sum(onehot * lookup, axis=-1)


def select_head(shard_heads, head_index):
    head_hits = (head_index[..., None] == jnp.arange(shard_heads.shape[-2])).astype(jnp.bfloat16)
    return jnp.einsum(
        "...hd,...h->...d", shard_heads, head_hits, preferred_element_type=jnp.float32
    ).astype(jnp.bfloat16)


def local(attention, out_weight, task_tags, delta_values, block_rows, block_columns, block_live):
    rows_count = attention.shape[0]
    width = out_weight.shape[1]
    head_dim = delta_values.shape[-1]
    per_shard = attention.shape[1] // head_dim
    owned_tasks = delta_values.shape[0]
    slot_count = delta_values.shape[1]
    col_blocks = width // head_dim
    owners = lax.axis_size("task")
    capacity = rows_count * 3 // 8
    owner_ids = task_tags // owned_tasks
    member = (owner_ids[:, None] == jnp.arange(owners)[None, :]).astype(jnp.int32)
    bucket_rank = jnp.sum(jnp.cumsum(member, axis=0) * member, axis=1) - 1
    placing = owner_ids * capacity + bucket_rank
    slot_tasks = (
        jnp.full((owners * capacity,), -1, jnp.int32)
        .at[placing]
        .set(task_tags - owner_ids * owned_tasks)
        .reshape(owners, capacity)
    )
    sending = (
        jnp.zeros((owners * capacity, attention.shape[1]), jnp.bfloat16).at[placing].set(attention)
    )
    sending = sending.reshape(owners, capacity, attention.shape[1])
    rows_in = lax.all_to_all(sending, "task", split_axis=0, concat_axis=0, tiled=True)
    task_ids = lax.all_to_all(slot_tasks, "task", split_axis=0, concat_axis=0, tiled=True)
    member_own = (task_ids[..., None] == jnp.arange(owned_tasks)).astype(jnp.int32)
    member_bf = member_own.astype(jnp.bfloat16)
    heads_in = rows_in.reshape(rows_in.shape[0], rows_in.shape[1], per_shard, head_dim)
    results = []
    found = []
    for slot_index in range(slot_count):
        chosen = select_head(heads_in, pick(block_rows[:, slot_index], member_own))
        spread = chosen[:, :, None, :] * member_bf[..., None]
        product = jnp.einsum(
            "abtd,tde->abe", spread, delta_values[:, slot_index], preferred_element_type=jnp.float32
        )
        results.append(
            product * pick(block_live[:, slot_index], member_own).astype(jnp.float32)[..., None]
        )
        found.append(pick(block_columns[:, slot_index], member_own))
    values_back = lax.all_to_all(
        jnp.stack(results, axis=2), "task", split_axis=0, concat_axis=0, tiled=True
    )
    columns_back = lax.all_to_all(
        jnp.stack(found, axis=2), "task", split_axis=0, concat_axis=0, tiled=True
    )
    values = values_back.reshape(owners * capacity, slot_count, head_dim)[placing]
    columns = columns_back.reshape(owners * capacity, slot_count)[placing]
    column_hits = (columns[:, :, None] == jnp.arange(col_blocks)).astype(jnp.float32)
    placed_delta = jnp.einsum(
        "rkc,rkd->cdr", column_hits, values, precision=lax.Precision.HIGHEST
    ).reshape(width, rows_count)
    base_part = lax.dot_general(
        out_weight, attention, (((0,), (1,)), ((), ())), preferred_element_type=jnp.float32
    )
    summed = lax.psum_scatter(base_part + placed_delta, "tensor", scatter_dimension=0, tiled=True)
    return summed.T.astype(jnp.bfloat16)


def solution(mesh):
    in_specs = (
        P(("groups", "task"), "tensor"),
        P("tensor", None),
        P(("groups", "task")),
        P("task", "tensor", None, None),
        P("task", "tensor"),
        P("task", "tensor"),
        P("task", "tensor"),
    )
    out_specs = P(("groups", "task"), "tensor")
    return jax.shard_map(local, mesh=mesh, in_specs=in_specs, out_specs=out_specs, check_vma=False)
```

profile of v0, /device:TPU:16, one launch (start us, length us, event | category | flops | bytes accessed | tf_op | source)
XLA Modules:
  0.0 324.8 jit_solution(9799497644414433075)
XLA Ops:
  6.5 0.7 multiply_subtract_fusion
  7.2 1.2 reduce-window.6
  8.5 0.2 slice_reduce_fusion
  8.7 0.2 reduce-window.9
  8.9 0.1 add_bitcast_fusion
  9.0 2.4 scatter_custom_fusion.1
  11.4 0.7 all_to_all.16
  12.1 3.2 all-to-all-start.1
  15.3 6.7 %scatter_custom_fusion = bf16[768,2048]{1,0:T(8,128)(2,1)} fusion(s32[512]{0:T(512)S(1)} %compare_select_fusion, bf16[512,2048]{1,0:T(8,128)(2,1)} %param.7, bf16[]{:T(256)} %constant.30.clone.1), kind=kCustom, calls=%fused_computation.18 | custom fusion | bytes 3146240 | tf_op jit(solution)/shard_map/scatter | solution.py:39
  22.1 0.0 all-to-all-done.1
  22.1 0.0 copy-start
  22.1 0.0 copy-start.1
  22.1 0.0 copy-start.2
  22.1 3.8 %all-to-all-start = ((bf16[4,192,2048]{2,1,0:T(8,128)(2,1)}), bf16[4,192,2048]{2,1,0:T(8,128)(2,1)S(1)}, u32[]{:S(2)}, u32[]{:S(2)}) async-start(bf16[4,192,2048]{2,1,0:T(8,128)(2,1)} %bitcast.101), calls=%async_computation | async-start | bytes 6291456 | tf_op jit(solution)/shard_map/all_to_all | solution.py:42
  25.9 0.0 copy-done
  26.0 0.0 copy-done.1
  26.0 0.0 copy-done.2
  26.0 0.2 select_reduce_fusion.1
  26.2 0.6 copy.22
  26.8 0.3 fusion.40
  27.1 35.7 %all-to-all-done = bf16[4,192,2048]{2,1,0:T(8,128)(2,1)S(1)} async-done(((bf16[4,192,2048]{2,1,0:T(8,128)(2,1)}), bf16[4,192,2048]{2,1,0:T(8,128)(2,1)S(1)}, u32[]{:S(2)}, u32[]{:S(2)}) %all-to-all-start) | async-done | bytes 3145760 | tf_op jit(solution)/shard_map/all_to_all | solution.py:42
  62.8 3.4 %all-to-all-start.3 = ((s32[4,192,2]{1,2,0:T(2,128)}), s32[4,192,2]{1,2,0:T(2,128)S(1)}, u32[]{:S(2)}, u32[]{:S(2)}) async-start(s32[4,192,2]{1,2,0:T(2,128)} %copy.22), calls=%async_computation.3 | async-start | bytes 16384 | tf_op jit(solution)/shard_map/all_to_all | solution.py:62
  66.3 1.0 copy.36
  67.3 1.0 fusion.2
  68.3 0.0 copy-start.4
  68.3 1.0 fusion
  69.3 0.1 copy-done.4
  69.5 1.8 fusion.31
  71.3 1.9 fusion.25
  73.2 0.1 pad_maximum_fusion
  73.3 0.9 copy.20
  74.2 0.0 all-to-all-done.3
  74.2 3.5 %all-to-all-start.2 = ((f32[4,192,2,128]{3,1,2,0:T(8,128)}), f32[4,192,2,128]{3,1,2,0:T(8,128)S(1)}, u32[]{:S(2)}, u32[]{:S(2)}) async-start(f32[4,192,2,128]{3,1,2,0:T(8,128)} %copy.20), calls=%async_computation.2 | async-start | bytes 1572864 | tf_op jit(solution)/shard_map/all_to_all | solution.py:59
  77.7 0.3 reduce-scatter.2.cloned.1.call-start
  78.0 0.2 copy.23
  78.2 1.0 gather_fusion.1
  79.2 10.1 %all-to-all-done.2 = f32[4,192,2,128]{3,1,2,0:T(8,128)S(1)} async-done(((f32[4,192,2,128]{3,1,2,0:T(8,128)}), f32[4,192,2,128]{3,1,2,0:T(8,128)S(1)}, u32[]{:S(2)}, u32[]{:S(2)}) %all-to-all-start.2) | async-done | bytes 786464 | tf_op jit(solution)/shard_map/all_to_all | solution.py:59
  89.3 0.6 copy.21
  89.9 2.1 gather_fusion
  92.0 12.4 %convolution_bitcast_fusion = f32[40,128,512]{1,0,2:T(8,128)} fusion(f32[512,2,128]{2,1,0:T(2,128)S(1)} %gather_fusion, s32[512,2]{1,0:T(8,128)S(1)} %gather_fusion.1), kind=kOutput, calls=%fused_computation.5 | convolution fusion | flops 62955520 | bytes 11014144 | tf_op jit(solution)/shard_map/rkc,rkd->cdr/dot_general | solution.py:68
  104.5 0.0 copy-start.3
  104.5 11.6 %copy.24 = f32[40,128,512]{2,1,0:T(8,128)} copy(f32[40,128,512]{1,0,2:T(8,128)} %convolution_bitcast_fusion) | data formatting | bytes 20971520 | tf_op jit(solution)/shard_map/rkc,rkd->cdr/transpose | solution.py:68
  116.0 0.0 copy-done.3
  116.0 19.2 %bitcast_add_fusion = f32[5120,512]{1,0:T(8,128)} fusion(f32[40,128,512]{2,1,0:T(8,128)} %copy.24, bf16[2048,5120]{1,0:T(8,128)(2,1)} %param.8, bf16[512,2048]{1,0:T(8,128)(2,1)S(1)} %copy-done.3), kind=kOutput, calls=%fused_computation.4 | convolution fusion | flops 10740039680 | bytes 44040192 | tf_op jit(solution)/shard_map/dot_general | solution.py:71
  135.2 0.0 reduce-scatter.2.cloned.1.call-update
  135.3 179.3 %reduce-scatter.2.cloned.1.call-done = f32[1280,512]{1,0:T(8,128)} async-done(((f32[5120,512]{1,0:T(8,128)}), f32[1280,512]{1,0:T(8,128)}) %reduce-scatter.2.cloned.1.call-update) | async-done | bytes 2621456 | tf_op jit(solution)/shard_map/reduce_scatter | solution.py:74
  314.6 1.9 convert_bitcast_fusion
  316.5 1.4 copy.25
  (14 shorter events, 0.1 us)
Async XLA Ops:
  12.1 10.0 %all-to-all-start.1 = ((s32[4,1,192]{2,1,0:T(1,128)}), s32[4,1,192]{2,1,0:T(1,128)S(1)}, u32[]{:S(2)}, u32[]{:S(2)}) async-start(s32[4,1,192]{2,1,0:T(1,128)} %all_to_all.16), calls=%async_computation.1 | async-start | bytes 8192 | tf_op jit(solution)/shard_map/all_to_all | solution.py:43
  22.1 3.9 %copy-start = (s32[16,2]{0,1:T(2,128)S(1)}, s32[16,2]{0,1:T(2,128)}, u32[]{:S(2)}) copy-start(s32[16,2]{0,1:T(2,128)} %param.11) | copy-start | bytes 388
  22.1 3.9 %copy-start.1 = (s32[16,2]{0,1:T(2,128)S(1)}, s32[16,2]{0,1:T(2,128)}, u32[]{:S(2)}) copy-start(s32[16,2]{0,1:T(2,128)} %param.12) | copy-start | bytes 388
  22.1 3.9 %copy-start.2 = (s32[16,2]{0,1:T(2,128)S(1)}, s32[16,2]{0,1:T(2,128)}, u32[]{:S(2)}) copy-start(s32[16,2]{0,1:T(2,128)} %param.13) | copy-start | bytes 388
  22.1 40.8 %all-to-all-start = ((bf16[4,192,2048]{2,1,0:T(8,128)(2,1)}), bf16[4,192,2048]{2,1,0:T(8,128)(2,1)S(1)}, u32[]{:S(2)}, u32[]{:S(2)}) async-start(bf16[4,192,2048]{2,1,0:T(8,128)(2,1)} %bitcast.101), calls=%async_computation | async-start | bytes 6291456 | tf_op jit(solution)/shard_map/all_to_all | solution.py:42
  62.8 11.4 %all-to-all-start.3 = ((s32[4,192,2]{1,2,0:T(2,128)}), s32[4,192,2]{1,2,0:T(2,128)S(1)}, u32[]{:S(2)}, u32[]{:S(2)}) async-start(s32[4,192,2]{1,2,0:T(2,128)} %copy.22), calls=%async_computation.3 | async-start | bytes 16384 | tf_op jit(solution)/shard_map/all_to_all | solution.py:62
  68.3 1.2 copy-start.4
  74.2 15.1 %all-to-all-start.2 = ((f32[4,192,2,128]{3,1,2,0:T(8,128)}), f32[4,192,2,128]{3,1,2,0:T(8,128)S(1)}, u32[]{:S(2)}, u32[]{:S(2)}) async-start(f32[4,192,2,128]{3,1,2,0:T(8,128)} %copy.20), calls=%async_computation.2 | async-start | bytes 1572864 | tf_op jit(solution)/shard_map/all_to_all | solution.py:59
  77.7 236.9 %reduce-scatter.2.cloned.1.call-start = ((), (), s32[]{:S(2)}) async-start(), calls=%async_computation.5 | async-start | bytes 13107200 | tf_op jit(solution)/shard_map/reduce_scatter | solution.py:74
  104.5 11.6 %copy-start.3 = (bf16[512,2048]{1,0:T(8,128)(2,1)S(1)}, bf16[512,2048]{1,0:T(8,128)(2,1)}, u32[]{:S(2)}) copy-start(bf16[512,2048]{1,0:T(8,128)(2,1)} %param.7) | copy-start | bytes 6291460
Sparse Core Ops, SparseCore 0:
  135.4 179.1 reduce-scatter.1
where the time goes:
time: 326 us; the launch traced here: 325 us
  waiting for transfers between devices  225 us (69%)
  matrix products  37.3 us (11%)
  local copies, waits for them, and re-layouts  29.7 us (9%)
  starting transfers between devices  14.3 us (4%)
  between operations  13.6 us (4%)
  other arithmetic  4.68 us (1%)
    reduce_scatter x1, waiting for transfers between devices, local(): lax.psum_scatter(base_part + placed_delta, 'tensor', scatter_dimension=0,...  179 us
    all_to_all x1, waiting for transfers between devices, local(): lax.all_to_all(sending, 'task', split_axis=0, concat_axis=0, tiled=True)  35.7 us
    dot_general x1, matrix products, local(): lax.dot_general(out_weight, attention, (((0,), (1,)), ((), ())), preferre...  19.2 us
    dot_general x1, matrix products, local(): jnp.einsum('rkc,rkd->cdr', column_hits, values, precision=lax.Precision.H...  12.4 us
    transpose x1, local copies, waits for them, and re-layouts, local(): jnp.einsum('rkc,rkd->cdr', column_hits, values, precision=lax.Precision.H...  11.6 us
    all_to_all x1, waiting for transfers between devices, local(): lax.all_to_all(jnp.stack(results, axis=2), 'task', split_axis=0, concat_a...  10.1 us
    scatter x1, local copies, waits for them, and re-layouts, local(): jnp.zeros((owners * capacity, attention.shape[1]), jnp.bfloat16).at[placing]  6.71 us
  transfers between devices with their start and end apart: 5, of which 3 were waited for; matrix products, arithmetic and copies ran while one was open for 5% of the time, Pallas kernels for 0%

commit v1 on v0

--- a/solution.py
+++ b/solution.py
@@ -1,6 +1,10 @@
+import functools
+
 import jax
 import jax.numpy as jnp
 from jax import lax
+from jax.experimental import pallas as pl
+from jax.experimental.pallas import tpu as pltpu
 from jax.sharding import PartitionSpec as P
 
 
@@ -15,7 +19,7 @@
     ).astype(jnp.bfloat16)
 
 
-def local(attention, out_weight, task_tags, delta_values, block_rows, block_columns, block_live):
+def local_general(attention, out_weight, task_tags, delta_values, block_rows, block_columns, block_live):
     rows_count = attention.shape[0]
     width = out_weight.shape[1]
     head_dim = delta_values.shape[-1]
@@ -75,6 +79,348 @@
     return summed.T.astype(jnp.bfloat16)
 
 
+MESH = pl.DeviceIdType.MESH
+PIECES = 4
+RING = 4
+WIDE = 256
+LEVELS = 32766.0
+
+
+def fits(mesh):
+    shards = mesh.shape["tensor"]
+    return 5120 % (shards * 256) == 0 and mesh.shape["groups"] == 2 and mesh.shape["task"] % 2 == 0
+
+
+def kernel(
+    n, owners, att_ref, w_ref, tag_ref, tab_ref, delta_ref, out_ref,
+    part, wbuf, tab_all, onehot_info, chosen, vals, dbuf, spread,
+    fsend, fscale, frecv, frscale, bsend, bscale, brecv, brscale,
+    wsem, tab_ssem, tab_rsem, own_ssem, own_rsem,
+    x_ssem, x_rsem, y_ssem, y_rsem, c_ssem, c_rsem,
+    f_ssem, f_rsem, fs_ssem, fs_rsem, b_ssem, b_rsem, bs_ssem, bs_rsem,
+):
+    rows = att_ref.shape[0]
+    blocks = part.shape[0]
+    per = blocks // n
+    g = lax.axis_index("groups")
+    t = lax.axis_index("task")
+    z = lax.axis_index("tensor")
+    twin = t + 1 - 2 * lax.rem(t, 2)
+    hops = range(2, owners, 2)
+    owned = tab_ref.shape[0]
+    steps = blocks * 128 // WIDE
+
+    def wcopy(i):
+        slot = lax.rem(i, RING)
+        return pltpu.make_async_copy(
+            w_ref.at[:, pl.ds(pl.multiple_of(i * WIDE, WIDE), WIDE)], wbuf.at[slot], wsem.at[slot]
+        )
+
+    for i in range(RING - 1):
+        wcopy(i).start()
+
+    barrier = pltpu.get_barrier_semaphore()
+    for k in range(1, owners):
+        pl.semaphore_signal(barrier, 1, device_id={"task": lax.rem(t + k, owners)}, device_id_type=MESH)
+    pl.semaphore_signal(barrier, 1, device_id={"groups": 1 - g}, device_id_type=MESH)
+
+    @pl.when(z > 0)
+    def _():
+        pl.semaphore_signal(barrier, 1, device_id={"tensor": z - 1}, device_id_type=MESH)
+
+    @pl.when(z < n - 1)
+    def _():
+        pl.semaphore_signal(barrier, 1, device_id={"tensor": z + 1}, device_id_type=MESH)
+
+    pl.semaphore_wait(barrier, owners + (z + n - 1) // n + (2 * n - 2 - z) // n)
+
+    def remote(src, dst, ssem, rsem, where):
+        return pltpu.make_async_remote_copy(
+            src_ref=src, dst_ref=dst, send_sem=ssem, recv_sem=rsem, device_id=where, device_id_type=MESH
+        )
+
+    def tab_copy(k):
+        here = tab_all.at[pl.ds(pl.multiple_of(t * owned, owned), owned)]
+        return remote(tab_ref, here, tab_ssem.at[k], tab_rsem.at[k], {"task": lax.rem(t + k, owners)})
+
+    def x_copy(h, q):
+        return remote(
+            delta_ref.at[g, q], dbuf.at[t, g, q], x_ssem.at[h, q], x_rsem.at[h, q],
+            {"task": lax.rem(t + 2 * h + 2, owners)},
+        )
+
+    def y_copy(h, q):
+        src = lax.rem(t - 2 * h - 2 + owners, owners)
+        return remote(
+            dbuf.at[src, g, q], dbuf.at[src, g, q], y_ssem.at[h, q], y_rsem.at[h, q], {"groups": 1 - g}
+        )
+
+    def c_copy(h, q, half):
+        src = lax.rem(t - 2 * h - 2 + owners, owners)
+        slot = g if half == 0 else 1 - g
+        return remote(
+            dbuf.at[src, slot, q], dbuf.at[src, slot, q], c_ssem.at[half, h, q], c_rsem.at[half, h, q],
+            {"task": twin},
+        )
+
+    own_copy = remote(delta_ref, dbuf.at[t], own_ssem, own_rsem, {"task": twin})
+    for k in range(1, owners):
+        tab_copy(k).start()
+    for q in range(PIECES):
+        for h in range(len(hops)):
+            x_copy(h, q).start()
+    own_copy.start()
+    tab_all[pl.ds(pl.multiple_of(t * owned, owned), owned), :] = tab_ref[...]
+
+    def base_step(i, carry):
+        @pl.when(i + RING - 1 < steps)
+        def _():
+            wcopy(i + RING - 1).start()
+
+        wcopy(i).wait()
+        got = jnp.dot(att_ref[...], wbuf[lax.rem(i, RING)], preferred_element_type=jnp.float32)
+        for e in range(WIDE // 128):
+            part[i * (WIDE // 128) + e] = got[:, e * 128 : (e + 1) * 128]
+        return carry
+
+    for q in range(PIECES):
+        lax.fori_loop(steps * q // PIECES, steps * (q + 1) // PIECES, base_step, 0)
+        for h in range(len(hops)):
+            x_copy(h, q).wait_recv()
+            y_copy(h, q).start()
+            c_copy(h, q, 0).start()
+
+    for k in range(1, owners):
+        tab_copy(k).wait_recv()
+    tasks = tab_all.shape[0]
+    hits = tag_ref[:, :tasks] == lax.broadcasted_iota(jnp.int32, (rows, tasks), 1)
+    onehot = jnp.where(hits, 1.0, 0.0).astype(jnp.bfloat16)
+    onehot_info[...] = jnp.dot(onehot, tab_all[...], preferred_element_type=jnp.float32)
+    tile = 64
+
+    def choose(i, carry):
+        at = pl.ds(pl.multiple_of(i * tile, tile), tile)
+        heads = [onehot_info[at, s * 128 : (s + 1) * 128] for s in range(2)]
+        picked = [jnp.zeros((tile, 128), jnp.float32) for s in range(2)]
+        for h in range(att_ref.shape[1] // 128):
+            block = att_ref[at, h * 128 : (h + 1) * 128].astype(jnp.float32)
+            for s in range(2):
+                picked[s] = jnp.where(heads[s] == float(h), block, picked[s])
+        for s in range(2):
+            chosen[s, at, :] = picked[s]
+        return carry
+
+    lax.fori_loop(0, rows // tile, choose, 0)
+    vals[...] = jnp.zeros_like(vals)
+
+    def add_piece(source, owner, s, q):
+        each = owned // PIECES
+        for e in range(each):
+            task = owner * owned + q * each + e
+            spread[:, e * 128 : (e + 1) * 128] = jnp.where(
+                tag_ref[...] == task, chosen[s], 0.0
+            ).astype(jnp.bfloat16)
+        vals[s] += jnp.dot(spread[...], source, preferred_element_type=jnp.float32)
+
+    def add_half(ref, owner, s):
+        def body(q, carry):
+            add_piece(ref[s, q], owner, s, q)
+            return carry
+
+        lax.fori_loop(0, PIECES, body, 0)
+
+    for s in range(2):
+        add_half(delta_ref, t, s)
+    own_copy.wait_recv()
+    for s in range(2):
+        add_half(dbuf.at[twin], twin, s)
+    for h in range(len(hops)):
+        src = lax.rem(t - 2 * h - 2 + owners, owners)
+        add_half(dbuf.at[src], src, g)
+    for q in range(PIECES):
+        for h in range(len(hops)):
+            y_copy(h, q).wait_recv()
+            c_copy(h, q, 1).start()
+    for h in range(len(hops)):
+        src = lax.rem(t - 2 * h - 2 + owners, owners)
+        add_half(dbuf.at[src], src, 1 - g)
+        other = lax.rem(twin - 2 * h - 2 + owners, owners)
+        for q in range(PIECES):
+            c_copy(h, q, 0).wait_recv()
+            c_copy(h, q, 1).wait_recv()
+        for s in range(2):
+            add_half(dbuf.at[other], other, s)
+    for s in range(2):
+        vals[s] = vals[s] * onehot_info[:, (4 + s) * 128 : (5 + s) * 128]
+
+    def block_sum(c):
+        total = part[c]
+        for s in range(2):
+            mine = onehot_info[:, (2 + s) * 128 : (3 + s) * 128] == c.astype(jnp.float32)
+            total = total + jnp.where(mine, vals[s], 0.0)
+        return total
+
+    def decoded(ref, scales, i):
+        whole = ref[i].astype(jnp.int32).astype(jnp.float32).reshape(rows // 8, 8, 128)
+        return (whole * scales[i][None]).reshape(rows, 128)
+
+    def encode(total, ref, scales, i):
+        cut = total.reshape(rows // 8, 8, 128)
+        top = jnp.maximum(jnp.max(jnp.abs(cut), axis=0), 1e-30)
+        scales[i] = top * (1.0 / LEVELS)
+        levels = jnp.round(cut * (LEVELS / top)[None]).reshape(rows, 128)
+        ref[i] = levels.astype(jnp.int32).astype(jnp.int16)
+
+    def f_copies(i):
+        where = {"tensor": z + 1}
+        return (
+            remote(fsend.at[i], frecv.at[i], f_ssem.at[i], f_rsem.at[i], where),
+            remote(fscale.at[i], frscale.at[i], fs_ssem.at[i], fs_rsem.at[i], where),
+        )
+
+    def b_copies(i):
+        where = {"tensor": z - 1}
+        return (
+            remote(bsend.at[i], brecv.at[i], b_ssem.at[i], b_rsem.at[i], where),
+            remote(bscale.at[i], brscale.at[i], bs_ssem.at[i], bs_rsem.at[i], where),
+        )
+
+    f_count = (n - 1 - z) * per
+    b_count = z * per
+
+    def chain(i, carry):
+        @pl.when(i < f_count)
+        def _():
+            part_at = (n - 1 - i // per) * per + i % per
+
+            @pl.when(z == 0)
+            def _():
+                encode(block_sum(part_at), fsend, fscale, i)
+
+            @pl.when(z > 0)
+            def _():
+                for copy in f_copies(i):
+                    copy.wait_recv()
+                encode(block_sum(part_at) + decoded(frecv, frscale, i), fsend, fscale, i)
+
+            for copy in f_copies(i):
+                copy.start()
+
+        @pl.when(i < b_count)
+        def _():
+            @pl.when(z == n - 1)
+            def _():
+                encode(block_sum(i), bsend, bscale, i)
+
+            @pl.when(z < n - 1)
+            def _():
+                for copy in b_copies(i):
+                    copy.wait_recv()
+                encode(block_sum(i) + decoded(brecv, brscale, i), bsend, bscale, i)
+
+            for copy in b_copies(i):
+                copy.start()
+
+        return carry
+
+    lax.fori_loop(0, (n - 1) * per, chain, 0)
+
+    def finish(j, carry):
+        part[z * per + j] = block_sum(z * per + j)
+
+        @pl.when(z < n - 1)
+        def _():
+            i = z * per + j
+            for copy in b_copies(i):
+                copy.wait_recv()
+            part[z * per + j] += decoded(brecv, brscale, i)
+
+        @pl.when(z > 0)
+        def _():
+            i = (n - 1 - z) * per + j
+            for copy in f_copies(i):
+                copy.wait_recv()
+            part[z * per + j] += decoded(frecv, frscale, i)
+
+        out_ref[:, pl.ds(pl.multiple_of(j * 128, 128), 128)] = part[z * per + j].astype(out_ref.dtype)
+        return carry
+
+    lax.fori_loop(0, per, finish, 0)
+
+    def drain(i, carry):
+        @pl.when(i < f_count)
+        def _():
+            for copy in f_copies(i):
+                copy.wait_send()
+
+        @pl.when(i < b_count)
+        def _():
+            for copy in b_copies(i):
+                copy.wait_send()
+
+        return carry
+
+    lax.fori_loop(0, (n - 1) * per, drain, 0)
+    for k in range(1, owners):
+        tab_copy(k).wait_send()
+    own_copy.wait_send()
+    for q in range(PIECES):
+        for h in range(len(hops)):
+            x_copy(h, q).wait_send()
+            y_copy(h, q).wait_send()
+            c_copy(h, q, 0).wait_send()
+            c_copy(h, q, 1).wait_send()
+
+
+def local_fast(sizes, attention, out_weight, task_tags, delta_values, block_rows, block_columns, block_live):
+    n, owners = sizes["tensor"], sizes["task"]
+    rows = attention.shape[0]
+    depth, width = out_weight.shape
+    owned, slots, hd = delta_values.shape[:3]
+    blocks = width // hd
+    chunk = width // n
+    count = (n - 1) * (blocks // n)
+    tags = jnp.broadcast_to(task_tags[:, None], (rows, 128))
+    info = jnp.concatenate([block_rows, block_columns, block_live], axis=1).astype(jnp.bfloat16)
+    table = jnp.broadcast_to(info[:, :, None], (owned, 3 * slots, 128)).reshape(owned, 3 * slots * 128)
+    deltas = delta_values.transpose(1, 0, 2, 3).reshape(slots, PIECES, owned // PIECES * hd, hd)
+    vmem = pl.BlockSpec(memory_space=pltpu.VMEM)
+    hop = max(owners // 2 - 1, 1)
+    dma = pltpu.SemaphoreType.DMA
+    sends = [
+        pltpu.VMEM((count, rows, 128), jnp.int16),
+        pltpu.VMEM((count, 8, 128), jnp.float32),
+    ]
+    return pl.pallas_call(
+        functools.partial(kernel, n, owners),
+        out_shape=jax.ShapeDtypeStruct((rows, chunk), jnp.bfloat16),
+        in_specs=[vmem, pl.BlockSpec(memory_space=pl.ANY), vmem, vmem, vmem],
+        out_specs=vmem,
+        scratch_shapes=[
+            pltpu.VMEM((blocks, rows, 128), jnp.float32),
+            pltpu.VMEM((RING, depth, WIDE), jnp.bfloat16),
+            pltpu.VMEM((owners * owned, 3 * slots * 128), jnp.bfloat16),
+            pltpu.VMEM((rows, 3 * slots * 128), jnp.float32),
+            pltpu.VMEM((slots, rows, 128), jnp.float32),
+            pltpu.VMEM((slots, rows, 128), jnp.float32),
+            pltpu.VMEM((owners, slots, PIECES, owned // PIECES * hd, hd), jnp.bfloat16),
+            pltpu.VMEM((rows, owned // PIECES * hd), jnp.bfloat16),
+            *(sends * 4),
+            dma((RING,)),
+            dma((owners,)), dma((owners,)), dma, dma,
+            dma((hop, PIECES)), dma((hop, PIECES)), dma((hop, PIECES)), dma((hop, PIECES)),
+            dma((2, hop, PIECES)), dma((2, hop, PIECES)),
+            *([dma((count,))] * 8),
+        ],
+        compiler_params=pltpu.CompilerParams(
+            collective_id=0, has_side_effects=True, vmem_limit_bytes=60 * 1024 * 1024
+        ),
+        cost_estimate=pl.CostEstimate(
+            flops=2 * rows * depth * width, bytes_accessed=2 * depth * width, transcendentals=0
+        ),
+    )(attention, out_weight, tags, table, deltas)
+
+
 def solution(mesh):
     in_specs = (
         P(("groups", "task"), "tensor"),
@@ -86,4 +432,6 @@
         P("task", "tensor"),
     )
     out_specs = P(("groups", "task"), "tensor")
+    fast = fits(mesh)
+    local = functools.partial(local_fast, mesh.shape) if fast else local_general
     return jax.shard_map(local, mesh=mesh, in_specs=in_specs, out_specs=out_specs, check_vma=False)

time: 326 us -> 163 us (0.50)
  waiting for transfers between devices: 225 us -> 0 us
  Pallas kernels: 0 us -> 153 us
  matrix products: 37.3 us -> 0 us
  local copies, waits for them, and re-layouts: 29.7 us -> 7.08 us
  starting transfers between devices: 14.3 us -> 0 us
  between operations: 13.6 us -> 0.02 us
    reduce_scatter x1 -> x0, waiting for transfers between devices: 179 us -> none  [local(): lax.psum_scatter(base_part + placed_delta, 'tensor', scatter_dimension=0,...]
    pallas_call x0 -> x1, Pallas kernels: none -> 153 us  [local_fast(): pl.pallas_call(functools.partial(kernel, n, owners), out_shape=jax.ShapeD...]
    all_to_all x4 -> x0, waiting for transfers between devices: 45.8 us -> none  [the longest x1 35.7 us: local(): lax.all_to_all(sending, 'task', split_axis=0, concat_axis=0, tiled=True)]
    dot_general x6 -> x0, matrix products: 37.3 us -> none  [the longest x1 19.2 us: local(): lax.dot_general(out_weight, attention, (((0,), (1,)), ((), ())), preferre...]
    all_to_all x4 -> x0, starting transfers between devices: 14 us -> none  [the longest x1 3.84 us: local(): lax.all_to_all(sending, 'task', split_axis=0, concat_axis=0, tiled=True)]
    transpose x1, local copies, waits for them, and re-layouts: 11.6 us -> 2.31 us  [local_fast(): delta_values.transpose(1, 0, 2, 3)]
    scatter x2 -> x0, local copies, waits for them, and re-layouts: 9.16 us -> none  [the longest x1 6.71 us: local(): jnp.zeros((owners * capacity, attention.shape[1]), jnp.bfloat16).at[placing]]
  transfers between devices with their start and end apart: 5 -> 0, of which waited for: 3 -> 0; matrix products, arithmetic and copies ran while one was open for 5% -> 0% of each run, Pallas kernels for 0% -> 0%
where the time goes in v1:
time: 163 us
  Pallas kernels  153 us (94%)
  local copies, waits for them, and re-layouts  7.08 us (4%)
  other arithmetic  2.06 us (1%)
    pallas_call x1, Pallas kernels, local_fast(): pl.pallas_call(functools.partial(kernel, n, owners), out_shape=jax.ShapeD...  153 us

profile of v1, /device:TPU:16, one launch (start us, length us, event | category | flops | bytes accessed | tf_op | source)
XLA Modules:
  0.0 162.6 jit_solution(16999450848259144935)
XLA Ops:
  0.0 0.7 convert.9
  0.7 0.7 convert.10
  1.4 0.7 convert.11
  2.1 0.1 copy.10
  2.2 0.1 broadcast_in_dim.5
  2.2 0.6 copy.14
  2.9 1.5 broadcast_in_dim.4.tag_ref
  4.4 2.3 %copy.11 = bf16[2,16,128,128]{3,2,1,0:T(8,128)(2,1)} copy(bf16[2,16,128,128]{3,2,0,1:T(8,128)(2,1)} %bitcast.6) | data formatting | bytes 2097152 | tf_op jit(solution)/shard_map/transpose | solution.py:386
  6.7 153.4 %shard_map.73 = bf16[512,1280]{1,0:T(8,128)(2,1)} custom-call(bf16[512,2048]{1,0:T(8,128)(2,1)} %att_ref.1, bf16[2048,5120]{1,0:T(8,128)(2,1)} %w_ref.1, s32[512,128]{1,0:T(8,128)} %broadcast_in_dim.4.tag_ref, bf16[16,768]{1,0:T(8,128)(2,1)} %bitcast.9, bf16[2,4,512,128]{3,2,1,0:T(8,128)(2,1)} %bitcast.7), custom_call_target="tpu_custom_call" | custom-call | flops 10737418240 | bytes 20971520 | tf_op jit(solution)/shard_map/pallas_call | solution.py:394
  160.1 2.5 %copy.16 = bf16[512,1280]{1,0:T(8,128)(2,1)} copy(bf16[512,1280]{1,0:T(8,128)(2,1)} %shard_map.73) | data formatting | bytes 2621440
  (1 shorter events, 0.0 us)

commit v2 on v1

--- a/solution.py
+++ b/solution.py
@@ -92,12 +92,14 @@
 
 
 def kernel(
-    n, owners, att_ref, w_ref, tag_ref, tab_ref, delta_ref, out_ref,
-    part, wbuf, tab_all, onehot_info, chosen, vals, dbuf, spread,
+    n, owners, att_ref, w_ref, tag_ref, row_ref, col_ref, live_ref, delta_ref, out_ref,
+    part, wbuf, tagf, tab, tab_all, ctab, ctab_in, onehot_info, chosen, vals, dbuf, spread,
+    vsend, vscale, vrecv, vrscale, far_vals, far_cols,
     fsend, fscale, frecv, frscale, bsend, bscale, brecv, brscale,
     wsem, tab_ssem, tab_rsem, own_ssem, own_rsem,
     x_ssem, x_rsem, y_ssem, y_rsem, c_ssem, c_rsem,
     f_ssem, f_rsem, fs_ssem, fs_rsem, b_ssem, b_rsem, bs_ssem, bs_rsem,
+    v_ssem, v_rsem, vs_ssem, vs_rsem, ct_ssem, ct_rsem,
 ):
     rows = att_ref.shape[0]
     blocks = part.shape[0]
@@ -107,13 +109,19 @@
     z = lax.axis_index("tensor")
     twin = t + 1 - 2 * lax.rem(t, 2)
     hops = range(2, owners, 2)
-    owned = tab_ref.shape[0]
+    owned = row_ref.shape[0]
     steps = blocks * 128 // WIDE
+    chunk_steps = steps // n
+    far = z // (n - 1)
+
+    def step_at(i):
+        return (i + chunk_steps * (n - 1) * (1 - far)) % steps
 
     def wcopy(i):
         slot = lax.rem(i, RING)
+        at = step_at(i)
         return pltpu.make_async_copy(
-            w_ref.at[:, pl.ds(pl.multiple_of(i * WIDE, WIDE), WIDE)], wbuf.at[slot], wsem.at[slot]
+            w_ref.at[:, pl.ds(pl.multiple_of(at * WIDE, WIDE), WIDE)], wbuf.at[slot], wsem.at[slot]
         )
 
     for i in range(RING - 1):
@@ -124,15 +132,9 @@
         pl.semaphore_signal(barrier, 1, device_id={"task": lax.rem(t + k, owners)}, device_id_type=MESH)
     pl.semaphore_signal(barrier, 1, device_id={"groups": 1 - g}, device_id_type=MESH)
 
-    @pl.when(z > 0)
-    def _():
-        pl.semaphore_signal(barrier, 1, device_id={"tensor": z - 1}, device_id_type=MESH)
-
-    @pl.when(z < n - 1)
-    def _():
-        pl.semaphore_signal(barrier, 1, device_id={"tensor": z + 1}, device_id_type=MESH)
-
-    pl.semaphore_wait(barrier, owners + (z + n - 1) // n + (2 * n - 2 - z) // n)
+    for k in range(1, n):
+        pl.semaphore_signal(barrier, 1, device_id={"tensor": lax.rem(z + k, n)}, device_id_type=MESH)
+    pl.semaphore_wait(barrier, owners + n - 1)
 
     def remote(src, dst, ssem, rsem, where):
         return pltpu.make_async_remote_copy(
@@ -141,7 +143,7 @@
 
     def tab_copy(k):
         here = tab_all.at[pl.ds(pl.multiple_of(t * owned, owned), owned)]
-        return remote(tab_ref, here, tab_ssem.at[k], tab_rsem.at[k], {"task": lax.rem(t + k, owners)})
+        return remote(tab, here, tab_ssem.at[k], tab_rsem.at[k], {"task": lax.rem(t + k, owners)})
 
     def x_copy(h, q):
         return remote(
@@ -162,6 +164,12 @@
             dbuf.at[src, slot, q], dbuf.at[src, slot, q], c_ssem.at[half, h, q], c_rsem.at[half, h, q],
             {"task": twin},
         )
+
+    for piece, ref in enumerate((row_ref, col_ref, live_ref)):
+        for s in range(2):
+            column = ref[:, s : s + 1].astype(jnp.float32)
+            at = (2 * piece + s) * 128
+            tab[:, at : at + 128] = jnp.broadcast_to(column, (owned, 128)).astype(jnp.bfloat16)
 
     own_copy = remote(delta_ref, dbuf.at[t], own_ssem, own_rsem, {"task": twin})
     for k in range(1, owners):
@@ -170,7 +178,7 @@
         for h in range(len(hops)):
             x_copy(h, q).start()
     own_copy.start()
-    tab_all[pl.ds(pl.multiple_of(t * owned, owned), owned), :] = tab_ref[...]
+    tab_all[pl.ds(pl.multiple_of(t * owned, owned), owned), :] = tab[...]
 
     def base_step(i, carry):
         @pl.when(i + RING - 1 < steps)
@@ -180,11 +188,53 @@
         wcopy(i).wait()
         got = jnp.dot(att_ref[...], wbuf[lax.rem(i, RING)], preferred_element_type=jnp.float32)
         for e in range(WIDE // 128):
-            part[i * (WIDE // 128) + e] = got[:, e * 128 : (e + 1) * 128]
+            part[step_at(i) * (WIDE // 128) + e] = got[:, e * 128 : (e + 1) * 128]
+        return carry
+
+    def decoded(ref, scales, i):
+        whole = ref[i].astype(jnp.int32).astype(jnp.float32).reshape(rows // 8, 8, 128)
+        return (whole * scales[i][None]).reshape(rows, 128)
+
+    def encode(total, ref, scales, i):
+        cut = total.reshape(rows // 8, 8, 128)
+        top = jnp.maximum(jnp.max(jnp.abs(cut), axis=0), 1e-30)
+        scales[i] = top * (1.0 / LEVELS)
+        levels = jnp.round(cut * (LEVELS / top)[None]).reshape(rows, 128)
+        ref[i] = levels.astype(jnp.int32).astype(jnp.int16)
+
+    def f_copies(i):
+        where = {"tensor": z + 1}
+        return (
+            remote(fsend.at[i], frecv.at[i], f_ssem.at[i], f_rsem.at[i], where),
+            remote(fscale.at[i], frscale.at[i], fs_ssem.at[i], fs_rsem.at[i], where),
+        )
+
+    def b_copies(i):
+        where = {"tensor": z - 1}
+        return (
+            remote(bsend.at[i], brecv.at[i], b_ssem.at[i], b_rsem.at[i], where),
+            remote(bscale.at[i], brscale.at[i], bs_ssem.at[i], bs_rsem.at[i], where),
+        )
+
+    def near_end(i, carry):
+        @pl.when(z == 0)
+        def _():
+            encode(part[(n - 1) * per + i], fsend, fscale, i)
+            for copy in f_copies(i):
+                copy.start()
+
+        @pl.when(z == n - 1)
+        def _():
+            encode(part[i], bsend, bscale, i)
+            for copy in b_copies(i):
+                copy.start()
+
         return carry
 
     for q in range(PIECES):
         lax.fori_loop(steps * q // PIECES, steps * (q + 1) // PIECES, base_step, 0)
+        if (q + 1) * n >= PIECES and q * n < PIECES:
+            lax.fori_loop(0, per, near_end, 0)
         for h in range(len(hops)):
             x_copy(h, q).wait_recv()
             y_copy(h, q).start()
@@ -193,8 +243,12 @@
     for k in range(1, owners):
         tab_copy(k).wait_recv()
     tasks = tab_all.shape[0]
-    hits = tag_ref[:, :tasks] == lax.broadcasted_iota(jnp.int32, (rows, tasks), 1)
+    for i in range(rows // 128):
+        line = jnp.broadcast_to(tag_ref[i : i + 1, :].astype(jnp.float32), (128, 128))
+        tagf[i * 128 : (i + 1) * 128, :] = line.T
+    hits = tagf[:, :tasks] == lax.broadcasted_iota(jnp.int32, (rows, tasks), 1).astype(jnp.float32)
     onehot = jnp.where(hits, 1.0, 0.0).astype(jnp.bfloat16)
+    ctab[...] = tab_all[:, 256:512]
     onehot_info[...] = jnp.dot(onehot, tab_all[...], preferred_element_type=jnp.float32)
     tile = 64
 
@@ -213,27 +267,27 @@
     lax.fori_loop(0, rows // tile, choose, 0)
     vals[...] = jnp.zeros_like(vals)
 
-    def add_piece(source, owner, s, q):
-        each = owned // PIECES
-        for e in range(each):
-            task = owner * owned + q * each + e
-            spread[:, e * 128 : (e + 1) * 128] = jnp.where(
-                tag_ref[...] == task, chosen[s], 0.0
-            ).astype(jnp.bfloat16)
-        vals[s] += jnp.dot(spread[...], source, preferred_element_type=jnp.float32)
-
-    def add_half(ref, owner, s):
+    def add_half(ref, owner, half):
+        each = owned // 2 // PIECES
+
         def body(q, carry):
-            add_piece(ref[s, q], owner, s, q)
+            for s in range(2):
+                for e in range(each):
+                    task = owner * owned + half * (owned // 2) + q * each + e
+                    spread[:, e * 128 : (e + 1) * 128] = jnp.where(
+                        tagf[...] == task.astype(jnp.float32), chosen[s], 0.0
+                    ).astype(jnp.bfloat16)
+                source = ref[half, q, :, s].reshape(each * 128, 128)
+                vals[s] += jnp.dot(spread[...], source, preferred_element_type=jnp.float32)
             return carry
 
         lax.fori_loop(0, PIECES, body, 0)
 
-    for s in range(2):
-        add_half(delta_ref, t, s)
+    for half in range(2):
+        add_half(delta_ref, t, half)
     own_copy.wait_recv()
-    for s in range(2):
-        add_half(dbuf.at[twin], twin, s)
+    for half in range(2):
+        add_half(dbuf.at[twin], twin, half)
     for h in range(len(hops)):
         src = lax.rem(t - 2 * h - 2 + owners, owners)
         add_half(dbuf.at[src], src, g)
@@ -248,10 +302,38 @@
         for q in range(PIECES):
             c_copy(h, q, 0).wait_recv()
             c_copy(h, q, 1).wait_recv()
-        for s in range(2):
-            add_half(dbuf.at[other], other, s)
+        for half in range(2):
+            add_half(dbuf.at[other], other, half)
     for s in range(2):
         vals[s] = vals[s] * onehot_info[:, (4 + s) * 128 : (5 + s) * 128]
+
+    for s in range(2):
+        encode(vals[s], vsend, vscale, s)
+
+    def v_copies(end):
+        where = {"tensor": end * (n - 1)}
+        return (
+            remote(vsend, vrecv.at[z], v_ssem.at[end], v_rsem.at[z], where),
+            remote(vscale, vrscale.at[z], vs_ssem.at[end], vs_rsem.at[z], where),
+            remote(ctab, ctab_in.at[z], ct_ssem.at[end], ct_rsem.at[z], where),
+        )
+
+    def v_arrivals(src):
+        return (
+            remote(vsend, vrecv.at[src], v_ssem.at[0], v_rsem.at[src], {"tensor": src}),
+            remote(vscale, vrscale.at[src], vs_ssem.at[0], vs_rsem.at[src], {"tensor": src}),
+            remote(ctab, ctab_in.at[src], ct_ssem.at[0], ct_rsem.at[src], {"tensor": src}),
+        )
+
+    @pl.when(z > 0)
+    def _():
+        for copy in v_copies(0):
+            copy.start()
+
+    @pl.when(z < n - 1)
+    def _():
+        for copy in v_copies(1):
+            copy.start()
 
     def block_sum(c):
         total = part[c]
@@ -260,73 +342,86 @@
             total = total + jnp.where(mine, vals[s], 0.0)
         return total
 
-    def decoded(ref, scales, i):
-        whole = ref[i].astype(jnp.int32).astype(jnp.float32).reshape(rows // 8, 8, 128)
-        return (whole * scales[i][None]).reshape(rows, 128)
-
-    def encode(total, ref, scales, i):
-        cut = total.reshape(rows // 8, 8, 128)
-        top = jnp.maximum(jnp.max(jnp.abs(cut), axis=0), 1e-30)
-        scales[i] = top * (1.0 / LEVELS)
-        levels = jnp.round(cut * (LEVELS / top)[None]).reshape(rows, 128)
-        ref[i] = levels.astype(jnp.int32).astype(jnp.int16)
-
-    def f_copies(i):
-        where = {"tensor": z + 1}
-        return (
-            remote(fsend.at[i], frecv.at[i], f_ssem.at[i], f_rsem.at[i], where),
-            remote(fscale.at[i], frscale.at[i], fs_ssem.at[i], fs_rsem.at[i], where),
-        )
-
-    def b_copies(i):
-        where = {"tensor": z - 1}
-        return (
-            remote(bsend.at[i], brecv.at[i], b_ssem.at[i], b_rsem.at[i], where),
-            remote(bscale.at[i], brscale.at[i], bs_ssem.at[i], bs_rsem.at[i], where),
-        )
-
     f_count = (n - 1 - z) * per
     b_count = z * per
 
-    def chain(i, carry):
+    def chain(first, i, carry):
         @pl.when(i < f_count)
         def _():
-            part_at = (n - 1 - i // per) * per + i % per
-
-            @pl.when(z == 0)
-            def _():
-                encode(block_sum(part_at), fsend, fscale, i)
+            at = (n - 1 - i // per) * per + i % per
+            base = (lambda: part[at]) if first else (lambda: block_sum(at))
 
             @pl.when(z > 0)
             def _():
                 for copy in f_copies(i):
                     copy.wait_recv()
-                encode(block_sum(part_at) + decoded(frecv, frscale, i), fsend, fscale, i)
-
-            for copy in f_copies(i):
-                copy.start()
+                encode(base() + decoded(frecv, frscale, i), fsend, fscale, i)
+                for copy in f_copies(i):
+                    copy.start()
+
+            if not first:
+                @pl.when(z == 0)
+                def _():
+                    encode(base(), fsend, fscale, i)
+                    for copy in f_copies(i):
+                        copy.start()
 
         @pl.when(i < b_count)
         def _():
-            @pl.when(z == n - 1)
-            def _():
-                encode(block_sum(i), bsend, bscale, i)
+            base = (lambda: part[i]) if first else (lambda: block_sum(i))
 
             @pl.when(z < n - 1)
             def _():
                 for copy in b_copies(i):
                     copy.wait_recv()
-                encode(block_sum(i) + decoded(brecv, brscale, i), bsend, bscale, i)
-
-            for copy in b_copies(i):
-                copy.start()
+                encode(base() + decoded(brecv, brscale, i), bsend, bscale, i)
+                for copy in b_copies(i):
+                    copy.start()
+
+            if not first:
+                @pl.when(z == n - 1)
+                def _():
+                    encode(base(), bsend, bscale, i)
+                    for copy in b_copies(i):
+                        copy.start()
 
         return carry
 
-    lax.fori_loop(0, (n - 1) * per, chain, 0)
+    lax.fori_loop(0, per, functools.partial(chain, True), 0)
+    lax.fori_loop(per, (n - 1) * per, functools.partial(chain, False), 0)
+
+    def far_source(end):
+        for k in range(n - 1):
+            src = k + 1 if end == 0 else k
+            for copy in v_arrivals(src):
+                copy.wait_recv()
+            for s in range(2):
+                whole = vrecv[src, s].astype(jnp.int32).astype(jnp.float32).reshape(rows // 8, 8, 128)
+                far_vals[k, s] = (whole * vrscale[src, s][None]).reshape(rows, 128)
+            far_cols[k] = jnp.dot(onehot_again(), ctab_in[src], preferred_element_type=jnp.float32)
+
+    def onehot_again():
+        found = tagf[:, :tasks] == lax.broadcasted_iota(jnp.int32, (rows, tasks), 1).astype(jnp.float32)
+        return jnp.where(found, 1.0, 0.0).astype(jnp.bfloat16)
+
+    @pl.when(z == 0)
+    def _():
+        far_source(0)
+
+    @pl.when(z == n - 1)
+    def _():
+        far_source(1)
 
     def finish(j, carry):
         part[z * per + j] = block_sum(z * per + j)
+
+        @pl.when((z == 0) | (z == n - 1))
+        def _():
+            at = (z * per + j).astype(jnp.float32)
+            for k in range(n - 1):
+                for s in range(2):
+                    there = far_cols[k, :, s * 128 : (s + 1) * 128] == at
+                    part[z * per + j] += jnp.where(there, far_vals[k, s], 0.0)
 
         @pl.when(z < n - 1)
         def _():
@@ -361,6 +456,16 @@
         return carry
 
     lax.fori_loop(0, (n - 1) * per, drain, 0)
+    @pl.when(z > 0)
+    def _():
+        for copy in v_copies(0):
+            copy.wait_send()
+
+    @pl.when(z < n - 1)
+    def _():
+        for copy in v_copies(1):
+            copy.wait_send()
+
     for k in range(1, owners):
         tab_copy(k).wait_send()
     own_copy.wait_send()
@@ -380,10 +485,8 @@
     blocks = width // hd
     chunk = width // n
     count = (n - 1) * (blocks // n)
-    tags = jnp.broadcast_to(task_tags[:, None], (rows, 128))
-    info = jnp.concatenate([block_rows, block_columns, block_live], axis=1).astype(jnp.bfloat16)
-    table = jnp.broadcast_to(info[:, :, None], (owned, 3 * slots, 128)).reshape(owned, 3 * slots * 128)
-    deltas = delta_values.transpose(1, 0, 2, 3).reshape(slots, PIECES, owned // PIECES * hd, hd)
+    tags = task_tags.reshape(rows // 128, 128)
+    deltas = delta_values.reshape(2, PIECES, owned // (2 * PIECES), slots, hd, hd)
     vmem = pl.BlockSpec(memory_space=pltpu.VMEM)
     hop = max(owners // 2 - 1, 1)
     dma = pltpu.SemaphoreType.DMA
@@ -394,23 +497,34 @@
     return pl.pallas_call(
         functools.partial(kernel, n, owners),
         out_shape=jax.ShapeDtypeStruct((rows, chunk), jnp.bfloat16),
-        in_specs=[vmem, pl.BlockSpec(memory_space=pl.ANY), vmem, vmem, vmem],
+        in_specs=[vmem, pl.BlockSpec(memory_space=pl.ANY), vmem, vmem, vmem, vmem, vmem],
         out_specs=vmem,
         scratch_shapes=[
             pltpu.VMEM((blocks, rows, 128), jnp.float32),
             pltpu.VMEM((RING, depth, WIDE), jnp.bfloat16),
+            pltpu.VMEM((rows, 128), jnp.float32),
+            pltpu.VMEM((owned, 3 * slots * 128), jnp.bfloat16),
             pltpu.VMEM((owners * owned, 3 * slots * 128), jnp.bfloat16),
+            pltpu.VMEM((owners * owned, slots * 128), jnp.bfloat16),
+            pltpu.VMEM((n, owners * owned, slots * 128), jnp.bfloat16),
             pltpu.VMEM((rows, 3 * slots * 128), jnp.float32),
             pltpu.VMEM((slots, rows, 128), jnp.float32),
             pltpu.VMEM((slots, rows, 128), jnp.float32),
-            pltpu.VMEM((owners, slots, PIECES, owned // PIECES * hd, hd), jnp.bfloat16),
-            pltpu.VMEM((rows, owned // PIECES * hd), jnp.bfloat16),
+            pltpu.VMEM((owners, *deltas.shape), jnp.bfloat16),
+            pltpu.VMEM((rows, owned // (2 * PIECES) * hd), jnp.bfloat16),
+            pltpu.VMEM((slots, rows, 128), jnp.int16),
+            pltpu.VMEM((slots, 8, 128), jnp.float32),
+            pltpu.VMEM((n, slots, rows, 128), jnp.int16),
+            pltpu.VMEM((n, slots, 8, 128), jnp.float32),
+            pltpu.VMEM((n - 1, slots, rows, 128), jnp.float32),
+            pltpu.VMEM((n - 1, rows, slots * 128), jnp.float32),
             *(sends * 4),
             dma((RING,)),
             dma((owners,)), dma((owners,)), dma, dma,
             dma((hop, PIECES)), dma((hop, PIECES)), dma((hop, PIECES)), dma((hop, PIECES)),
             dma((2, hop, PIECES)), dma((2, hop, PIECES)),
             *([dma((count,))] * 8),
+            *([dma((2,)), dma((n,))] * 3),
         ],
         compiler_params=pltpu.CompilerParams(
             collective_id=0, has_side_effects=True, vmem_limit_bytes=60 * 1024 * 1024
@@ -418,7 +532,7 @@
         cost_estimate=pl.CostEstimate(
             flops=2 * rows * depth * width, bytes_accessed=2 * depth * width, transcendentals=0
         ),
-    )(attention, out_weight, tags, table, deltas)
+    )(attention, out_weight, tags, block_rows, block_columns, block_live, deltas)
 
 
 def solution(mesh):

time: 163 us -> 169 us (1.037)
  Pallas kernels: 153 us -> 162 us
  other arithmetic: 2.06 us -> 0 us
    pallas_call x1, Pallas kernels: 153 us -> 162 us  [local_fast(): pl.pallas_call(functools.partial(kernel, n, owners), out_shape=jax.ShapeD...]
    unnamed x2 -> x4, local copies, waits for them, and re-layouts: 3.06 us -> 6.51 us
    transpose x1 -> x0, local copies, waits for them, and re-layouts: 2.31 us -> none  [local_fast(): delta_values.transpose(1, 0, 2, 3)]
    another operation x3 -> x0, other arithmetic: 2.04 us -> none
where the time goes in v2:
time: 169 us
  Pallas kernels  162 us (96%)
  local copies, waits for them, and re-layouts  6.51 us (4%)
    pallas_call x1, Pallas kernels, local_fast(): pl.pallas_call(functools.partial(kernel, n, owners), out_shape=jax.ShapeD...  162 us
    unnamed x4, local copies, waits for them, and re-layouts  6.51 us

profile of v2, /device:TPU:16, one launch (start us, length us, event | category | flops | bytes accessed | tf_op | source)
XLA Modules:
  0.0 168.8 jit_solution(3190834859866969214)
XLA Ops:
  0.0 1.4 copy.8.row_ref
  1.4 1.4 copy.9.col_ref
  2.7 1.3 copy.10.live_ref
  4.1 162.3 %shard_map.73 = bf16[512,1280]{1,0:T(8,128)(2,1)} custom-call(bf16[512,2048]{1,0:T(8,128)(2,1)} %att_ref.1, bf16[2048,5120]{1,0:T(8,128)(2,1)} %w_ref.1, s32[4,128]{1,0:T(4,128)} %bitcast.3, s32[16,2]{1,0:T(8,128)} %copy.8.row_ref, s32[16,2]{1,0:T(8,128)} %copy.9.col_ref, s32[16,2]{1,0:T(8,128)} %copy.10.live_ref, bf16[2,4,2,2,128,128]{5,4,3,2,1,0:T(8,128)(2,1)} %bitcast.2), custom_call_target="tpu_custom_call" | custom-call | flops 10737418240 | bytes 20971520 | tf_op jit(solution)/shard_map/pallas_call | solution.py:497
  166.3 2.5 %copy.12 = bf16[512,1280]{1,0:T(8,128)(2,1)} copy(bf16[512,1280]{1,0:T(8,128)(2,1)} %shard_map.73) | data formatting | bytes 2621440

commit v3 on v2

--- a/solution.py
+++ b/solution.py
@@ -84,11 +84,12 @@
 RING = 4
 WIDE = 256
 LEVELS = 32766.0
+PAIR = WIDE // 128
 
 
 def fits(mesh):
     shards = mesh.shape["tensor"]
-    return 5120 % (shards * 256) == 0 and mesh.shape["groups"] == 2 and mesh.shape["task"] % 2 == 0
+    return shards > 1 and 5120 % (shards * 256) == 0 and mesh.shape["groups"] == 2 and mesh.shape["task"] % 2 == 0
 
 
 def kernel(
@@ -102,20 +103,18 @@
     v_ssem, v_rsem, vs_ssem, vs_rsem, ct_ssem, ct_rsem,
 ):
     rows = att_ref.shape[0]
-    blocks = part.shape[0]
-    per = blocks // n
+    steps = part.shape[0]
+    per = steps // n
     g = lax.axis_index("groups")
     t = lax.axis_index("task")
     z = lax.axis_index("tensor")
     twin = t + 1 - 2 * lax.rem(t, 2)
     hops = range(2, owners, 2)
     owned = row_ref.shape[0]
-    steps = blocks * 128 // WIDE
-    chunk_steps = steps // n
     far = z // (n - 1)
 
     def step_at(i):
-        return (i + chunk_steps * (n - 1) * (1 - far)) % steps
+        return (i + per * (n - 1) * (1 - far)) % steps
 
     def wcopy(i):
         slot = lax.rem(i, RING)
@@ -187,20 +186,20 @@
 
         wcopy(i).wait()
         got = jnp.dot(att_ref[...], wbuf[lax.rem(i, RING)], preferred_element_type=jnp.float32)
-        for e in range(WIDE // 128):
-            part[step_at(i) * (WIDE // 128) + e] = got[:, e * 128 : (e + 1) * 128]
+        for e in range(PAIR):
+            part[step_at(i), e] = got[:, e * 128 : (e + 1) * 128]
         return carry
 
-    def decoded(ref, scales, i):
-        whole = ref[i].astype(jnp.int32).astype(jnp.float32).reshape(rows // 8, 8, 128)
-        return (whole * scales[i][None]).reshape(rows, 128)
-
-    def encode(total, ref, scales, i):
+    def decoded(blocks, scale):
+        whole = blocks.astype(jnp.int32).astype(jnp.float32).reshape(rows // 8, 8, 128)
+        return (whole * scale[None]).reshape(rows, 128)
+
+    def encode(total, ref, scales, at):
         cut = total.reshape(rows // 8, 8, 128)
         top = jnp.maximum(jnp.max(jnp.abs(cut), axis=0), 1e-30)
-        scales[i] = top * (1.0 / LEVELS)
+        scales[at] = top * (1.0 / LEVELS)
         levels = jnp.round(cut * (LEVELS / top)[None]).reshape(rows, 128)
-        ref[i] = levels.astype(jnp.int32).astype(jnp.int16)
+        ref[at] = levels.astype(jnp.int32).astype(jnp.int16)
 
     def f_copies(i):
         where = {"tensor": z + 1}
@@ -219,13 +218,15 @@
     def near_end(i, carry):
         @pl.when(z == 0)
         def _():
-            encode(part[(n - 1) * per + i], fsend, fscale, i)
+            for e in range(PAIR):
+                encode(part[(n - 1) * per + i, e], fsend, fscale, (i, e))
             for copy in f_copies(i):
                 copy.start()
 
         @pl.when(z == n - 1)
         def _():
-            encode(part[i], bsend, bscale, i)
+            for e in range(PAIR):
+                encode(part[i, e], bsend, bscale, (i, e))
             for copy in b_copies(i):
                 copy.start()
 
@@ -335,10 +336,11 @@
         for copy in v_copies(1):
             copy.start()
 
-    def block_sum(c):
-        total = part[c]
+    def block_sum(c, e):
+        total = part[c, e]
+        block = (c * PAIR + e).astype(jnp.float32)
         for s in range(2):
-            mine = onehot_info[:, (2 + s) * 128 : (3 + s) * 128] == c.astype(jnp.float32)
+            mine = onehot_info[:, (2 + s) * 128 : (3 + s) * 128] == block
             total = total + jnp.where(mine, vals[s], 0.0)
         return total
 
@@ -349,39 +351,43 @@
         @pl.when(i < f_count)
         def _():
             at = (n - 1 - i // per) * per + i % per
-            base = (lambda: part[at]) if first else (lambda: block_sum(at))
+            base = (lambda e: part[at, e]) if first else (lambda e: block_sum(at, e))
 
             @pl.when(z > 0)
             def _():
                 for copy in f_copies(i):
                     copy.wait_recv()
-                encode(base() + decoded(frecv, frscale, i), fsend, fscale, i)
+                for e in range(PAIR):
+                    encode(base(e) + decoded(frecv[i, e], frscale[i, e]), fsend, fscale, (i, e))
                 for copy in f_copies(i):
                     copy.start()
 
             if not first:
                 @pl.when(z == 0)
                 def _():
-                    encode(base(), fsend, fscale, i)
+                    for e in range(PAIR):
+                        encode(base(e), fsend, fscale, (i, e))
                     for copy in f_copies(i):
                         copy.start()
 
         @pl.when(i < b_count)
         def _():
-            base = (lambda: part[i]) if first else (lambda: block_sum(i))
+            base = (lambda e: part[i, e]) if first else (lambda e: block_sum(i, e))
 
             @pl.when(z < n - 1)
             def _():
                 for copy in b_copies(i):
                     copy.wait_recv()
-                encode(base() + decoded(brecv, brscale, i), bsend, bscale, i)
+                for e in range(PAIR):
+                    encode(base(e) + decoded(brecv[i, e], brscale[i, e]), bsend, bscale, (i, e))
                 for copy in b_copies(i):
                     copy.start()
 
             if not first:
                 @pl.when(z == n - 1)
                 def _():
-                    encode(base(), bsend, bscale, i)
+                    for e in range(PAIR):
+                        encode(base(e), bsend, bscale, (i, e))
                     for copy in b_copies(i):
                         copy.start()
 
@@ -396,8 +402,7 @@
             for copy in v_arrivals(src):
                 copy.wait_recv()
             for s in range(2):
-                whole = vrecv[src, s].astype(jnp.int32).astype(jnp.float32).reshape(rows // 8, 8, 128)
-                far_vals[k, s] = (whole * vrscale[src, s][None]).reshape(rows, 128)
+                far_vals[k, s] = decoded(vrecv[src, s], vrscale[src, s])
             far_cols[k] = jnp.dot(onehot_again(), ctab_in[src], preferred_element_type=jnp.float32)
 
     def onehot_again():
@@ -413,31 +418,38 @@
         far_source(1)
 
     def finish(j, carry):
-        part[z * per + j] = block_sum(z * per + j)
+        c = z * per + j
+        for e in range(PAIR):
+            part[c, e] = block_sum(c, e)
 
         @pl.when((z == 0) | (z == n - 1))
         def _():
-            at = (z * per + j).astype(jnp.float32)
-            for k in range(n - 1):
-                for s in range(2):
-                    there = far_cols[k, :, s * 128 : (s + 1) * 128] == at
-                    part[z * per + j] += jnp.where(there, far_vals[k, s], 0.0)
+            for e in range(PAIR):
+                block = (c * PAIR + e).astype(jnp.float32)
+                for k in range(n - 1):
+                    for s in range(2):
+                        there = far_cols[k, :, s * 128 : (s + 1) * 128] == block
+                        part[c, e] += jnp.where(there, far_vals[k, s], 0.0)
 
         @pl.when(z < n - 1)
         def _():
             i = z * per + j
             for copy in b_copies(i):
                 copy.wait_recv()
-            part[z * per + j] += decoded(brecv, brscale, i)
+            for e in range(PAIR):
+                part[c, e] += decoded(brecv[i, e], brscale[i, e])
 
         @pl.when(z > 0)
         def _():
             i = (n - 1 - z) * per + j
             for copy in f_copies(i):
                 copy.wait_recv()
-            part[z * per + j] += decoded(frecv, frscale, i)
-
-        out_ref[:, pl.ds(pl.multiple_of(j * 128, 128), 128)] = part[z * per + j].astype(out_ref.dtype)
+            for e in range(PAIR):
+                part[c, e] += decoded(frecv[i, e], frscale[i, e])
+
+        for e in range(PAIR):
+            at = pl.ds(pl.multiple_of(j * WIDE + e * 128, 128), 128)
+            out_ref[:, at] = part[c, e].astype(out_ref.dtype)
         return carry
 
     lax.fori_loop(0, per, finish, 0)
@@ -482,17 +494,17 @@
     rows = attention.shape[0]
     depth, width = out_weight.shape
     owned, slots, hd = delta_values.shape[:3]
-    blocks = width // hd
+    steps = width // WIDE
     chunk = width // n
-    count = (n - 1) * (blocks // n)
+    count = (n - 1) * (steps // n)
     tags = task_tags.reshape(rows // 128, 128)
     deltas = delta_values.reshape(2, PIECES, owned // (2 * PIECES), slots, hd, hd)
     vmem = pl.BlockSpec(memory_space=pltpu.VMEM)
     hop = max(owners // 2 - 1, 1)
     dma = pltpu.SemaphoreType.DMA
     sends = [
-        pltpu.VMEM((count, rows, 128), jnp.int16),
-        pltpu.VMEM((count, 8, 128), jnp.float32),
+        pltpu.VMEM((count, PAIR, rows, 128), jnp.int16),
+        pltpu.VMEM((count, PAIR, 8, 128), jnp.float32),
     ]
     return pl.pallas_call(
         functools.partial(kernel, n, owners),
@@ -500,7 +512,7 @@
         in_specs=[vmem, pl.BlockSpec(memory_space=pl.ANY), vmem, vmem, vmem, vmem, vmem],
         out_specs=vmem,
         scratch_shapes=[
-            pltpu.VMEM((blocks, rows, 128), jnp.float32),
+            pltpu.VMEM((steps, PAIR, rows, 128), jnp.float32),
             pltpu.VMEM((RING, depth, WIDE), jnp.bfloat16),
             pltpu.VMEM((rows, 128), jnp.float32),
             pltpu.VMEM((owned, 3 * slots * 128), jnp.bfloat16),

time: 169 us -> 149 us (0.88)
  Pallas kernels: 162 us -> 141 us
    pallas_call x1, Pallas kernels: 162 us -> 141 us  [local_fast(): pl.pallas_call(functools.partial(kernel, n, owners), out_shape=jax.ShapeD...]
where the time goes in v3:
time: 149 us; the launch traced here: 148 us
  Pallas kernels  141 us (95%)
  local copies, waits for them, and re-layouts  6.51 us (4%)
    pallas_call x1, Pallas kernels, local_fast(): pl.pallas_call(functools.partial(kernel, n, owners), out_shape=jax.ShapeD...  141 us
    unnamed x4, local copies, waits for them, and re-layouts  6.51 us

profile of v3, /device:TPU:16, one launch (start us, length us, event | category | flops | bytes accessed | tf_op | source)
XLA Modules:
  0.0 147.6 jit_solution(12954417486208384421)
XLA Ops:
  0.0 1.4 copy.8.row_ref
  1.4 1.4 copy.9.col_ref
  2.7 1.3 copy.10.live_ref
  4.1 141.1 %shard_map.73 = bf16[512,1280]{1,0:T(8,128)(2,1)} custom-call(bf16[512,2048]{1,0:T(8,128)(2,1)} %att_ref.1, bf16[2048,5120]{1,0:T(8,128)(2,1)} %w_ref.1, s32[4,128]{1,0:T(4,128)} %bitcast.3, s32[16,2]{1,0:T(8,128)} %copy.8.row_ref, s32[16,2]{1,0:T(8,128)} %copy.9.col_ref, s32[16,2]{1,0:T(8,128)} %copy.10.live_ref, bf16[2,4,2,2,128,128]{5,4,3,2,1,0:T(8,128)(2,1)} %bitcast.2), custom_call_target="tpu_custom_call" | custom-call | flops 10737418240 | bytes 20971520 | tf_op jit(solution)/shard_map/pallas_call | solution.py:509
  145.2 2.5 %copy.12 = bf16[512,1280]{1,0:T(8,128)(2,1)} copy(bf16[512,1280]{1,0:T(8,128)(2,1)} %shard_map.73) | data formatting | bytes 2621440

commit v4 on v3

--- a/solution.py
+++ b/solution.py
@@ -219,7 +219,7 @@
         @pl.when(z == 0)
         def _():
             for e in range(PAIR):
-                encode(part[(n - 1) * per + i, e], fsend, fscale, (i, e))
+                encode(part[(n - 1 - i // per) * per + i % per, e], fsend, fscale, (i, e))
             for copy in f_copies(i):
                 copy.start()
 
@@ -240,6 +240,8 @@
             x_copy(h, q).wait_recv()
             y_copy(h, q).start()
             c_copy(h, q, 0).start()
+
+    lax.fori_loop(per, (n - 1) * per, near_end, 0)
 
     for k in range(1, owners):
         tab_copy(k).wait_recv()
@@ -311,12 +313,12 @@
     for s in range(2):
         encode(vals[s], vsend, vscale, s)
 
-    def v_copies(end):
-        where = {"tensor": end * (n - 1)}
+    def v_copies(k):
+        where = {"tensor": lax.rem(z + k, n)}
         return (
-            remote(vsend, vrecv.at[z], v_ssem.at[end], v_rsem.at[z], where),
-            remote(vscale, vrscale.at[z], vs_ssem.at[end], vs_rsem.at[z], where),
-            remote(ctab, ctab_in.at[z], ct_ssem.at[end], ct_rsem.at[z], where),
+            remote(vsend, vrecv.at[z], v_ssem.at[k], v_rsem.at[z], where),
+            remote(vscale, vrscale.at[z], vs_ssem.at[k], vs_rsem.at[z], where),
+            remote(ctab, ctab_in.at[z], ct_ssem.at[k], ct_rsem.at[z], where),
         )
 
     def v_arrivals(src):
@@ -326,14 +328,8 @@
             remote(ctab, ctab_in.at[src], ct_ssem.at[0], ct_rsem.at[src], {"tensor": src}),
         )
 
-    @pl.when(z > 0)
-    def _():
-        for copy in v_copies(0):
-            copy.start()
-
-    @pl.when(z < n - 1)
-    def _():
-        for copy in v_copies(1):
+    for k in range(1, n):
+        for copy in v_copies(k):
             copy.start()
 
     def block_sum(c, e):
@@ -347,89 +343,49 @@
     f_count = (n - 1 - z) * per
     b_count = z * per
 
-    def chain(first, i, carry):
-        @pl.when(i < f_count)
+    def chain(i, carry):
+        @pl.when((i < f_count) & (z > 0))
         def _():
             at = (n - 1 - i // per) * per + i % per
-            base = (lambda e: part[at, e]) if first else (lambda e: block_sum(at, e))
-
-            @pl.when(z > 0)
-            def _():
-                for copy in f_copies(i):
-                    copy.wait_recv()
-                for e in range(PAIR):
-                    encode(base(e) + decoded(frecv[i, e], frscale[i, e]), fsend, fscale, (i, e))
-                for copy in f_copies(i):
-                    copy.start()
-
-            if not first:
-                @pl.when(z == 0)
-                def _():
-                    for e in range(PAIR):
-                        encode(base(e), fsend, fscale, (i, e))
-                    for copy in f_copies(i):
-                        copy.start()
-
-        @pl.when(i < b_count)
-        def _():
-            base = (lambda e: part[i, e]) if first else (lambda e: block_sum(i, e))
-
-            @pl.when(z < n - 1)
-            def _():
-                for copy in b_copies(i):
-                    copy.wait_recv()
-                for e in range(PAIR):
-                    encode(base(e) + decoded(brecv[i, e], brscale[i, e]), bsend, bscale, (i, e))
-                for copy in b_copies(i):
-                    copy.start()
-
-            if not first:
-                @pl.when(z == n - 1)
-                def _():
-                    for e in range(PAIR):
-                        encode(base(e), bsend, bscale, (i, e))
-                    for copy in b_copies(i):
-                        copy.start()
+            for copy in f_copies(i):
+                copy.wait_recv()
+            for e in range(PAIR):
+                encode(part[at, e] + decoded(frecv[i, e], frscale[i, e]), fsend, fscale, (i, e))
+            for copy in f_copies(i):
+                copy.start()
+
+        @pl.when((i < b_count) & (z < n - 1))
+        def _():
+            for copy in b_copies(i):
+                copy.wait_recv()
+            for e in range(PAIR):
+                encode(part[i, e] + decoded(brecv[i, e], brscale[i, e]), bsend, bscale, (i, e))
+            for copy in b_copies(i):
+                copy.start()
 
         return carry
 
-    lax.fori_loop(0, per, functools.partial(chain, True), 0)
-    lax.fori_loop(per, (n - 1) * per, functools.partial(chain, False), 0)
-
-    def far_source(end):
-        for k in range(n - 1):
-            src = k + 1 if end == 0 else k
-            for copy in v_arrivals(src):
-                copy.wait_recv()
-            for s in range(2):
-                far_vals[k, s] = decoded(vrecv[src, s], vrscale[src, s])
-            far_cols[k] = jnp.dot(onehot_again(), ctab_in[src], preferred_element_type=jnp.float32)
-
-    def onehot_again():
-        found = tagf[:, :tasks] == lax.broadcasted_iota(jnp.int32, (rows, tasks), 1).astype(jnp.float32)
-        return jnp.where(found, 1.0, 0.0).astype(jnp.bfloat16)
-
-    @pl.when(z == 0)
-    def _():
-        far_source(0)
-
-    @pl.when(z == n - 1)
-    def _():
-        far_source(1)
+    lax.fori_loop(0, (n - 1) * per, chain, 0)
+
+    for k in range(1, n):
+        src = lax.rem(z + k, n)
+        for copy in v_arrivals(src):
+            copy.wait_recv()
+        for s in range(2):
+            far_vals[k - 1, s] = decoded(vrecv[src, s], vrscale[src, s])
+        far_cols[k - 1] = jnp.dot(onehot, ctab_in[src], preferred_element_type=jnp.float32)
 
     def finish(j, carry):
         c = z * per + j
         for e in range(PAIR):
             part[c, e] = block_sum(c, e)
 
-        @pl.when((z == 0) | (z == n - 1))
-        def _():
-            for e in range(PAIR):
-                block = (c * PAIR + e).astype(jnp.float32)
-                for k in range(n - 1):
-                    for s in range(2):
-                        there = far_cols[k, :, s * 128 : (s + 1) * 128] == block
-                        part[c, e] += jnp.where(there, far_vals[k, s], 0.0)
+        for e in range(PAIR):
+            block = (c * PAIR + e).astype(jnp.float32)
+            for k in range(n - 1):
+                for s in range(2):
+                    there = far_cols[k, :, s * 128 : (s + 1) * 128] == block
+                    part[c, e] += jnp.where(there, far_vals[k, s], 0.0)
 
         @pl.when(z < n - 1)
         def _():
@@ -468,14 +424,8 @@
         return carry
 
     lax.fori_loop(0, (n - 1) * per, drain, 0)
-    @pl.when(z > 0)
-    def _():
-        for copy in v_copies(0):
-            copy.wait_send()
-
-    @pl.when(z < n - 1)
-    def _():
-        for copy in v_copies(1):
+    for k in range(1, n):
+        for copy in v_copies(k):
             copy.wait_send()
 
     for k in range(1, owners):
@@ -536,7 +486,7 @@
             dma((hop, PIECES)), dma((hop, PIECES)), dma((hop, PIECES)), dma((hop, PIECES)),
             dma((2, hop, PIECES)), dma((2, hop, PIECES)),
             *([dma((count,))] * 8),
-            *([dma((2,)), dma((n,))] * 3),
+            *([dma((n,))] * 6),
         ],
         compiler_params=pltpu.CompilerParams(
             collective_id=0, has_side_effects=True, vmem_limit_bytes=60 * 1024 * 1024

time: 149 us -> 160 us (1.074)
  Pallas kernels: 141 us -> 154 us
    pallas_call x1, Pallas kernels: 141 us -> 154 us  [local_fast(): pl.pallas_call(functools.partial(kernel, n, owners), out_shape=jax.ShapeD...]
where the time goes in v4:
time: 160 us
  Pallas kernels  154 us (96%)
  local copies, waits for them, and re-layouts  6.51 us (4%)
    pallas_call x1, Pallas kernels, local_fast(): pl.pallas_call(functools.partial(kernel, n, owners), out_shape=jax.ShapeD...  154 us
    unnamed x4, local copies, waits for them, and re-layouts  6.51 us

profile of v4, /device:TPU:16, one launch (start us, length us, event | category | flops | bytes accessed | tf_op | source)
XLA Modules:
  0.0 160.2 jit_solution(10405894614443552435)
XLA Ops:
  0.0 1.4 copy.8.row_ref
  1.4 1.4 copy.9.col_ref
  2.7 1.3 copy.10.live_ref
  4.1 153.7 %shard_map.73 = bf16[512,1280]{1,0:T(8,128)(2,1)} custom-call(bf16[512,2048]{1,0:T(8,128)(2,1)} %att_ref.1, bf16[2048,5120]{1,0:T(8,128)(2,1)} %w_ref.1, s32[4,128]{1,0:T(4,128)} %bitcast.3, s32[16,2]{1,0:T(8,128)} %copy.8.row_ref, s32[16,2]{1,0:T(8,128)} %copy.9.col_ref, s32[16,2]{1,0:T(8,128)} %copy.10.live_ref, bf16[2,4,2,2,128,128]{5,4,3,2,1,0:T(8,128)(2,1)} %bitcast.2), custom_call_target="tpu_custom_call" | custom-call | flops 10737418240 | bytes 20971520 | tf_op jit(solution)/shard_map/pallas_call | solution.py:459
  157.7 2.5 %copy.12 = bf16[512,1280]{1,0:T(8,128)(2,1)} copy(bf16[512,1280]{1,0:T(8,128)(2,1)} %shard_map.73) | data formatting | bytes 2621440
